TPU v7x, 256 devices: a whole 4x4x8 slice. The times are simulated.
256 devices in a mesh: ctx: 64 (over y, z, core), mp: 4 (over x).
Axes of the slice: x: 4, y: 4, z: 8, core: 2. Of those that a mesh axis runs over, the one named last changes fastest.
Arguments:
- hidden: bfloat16 [8192, 4096], P('ctx', 'mp'), may hold values from -6 to 6
- queries: bfloat16 [8192, 4096], P('ctx', 'mp'), may hold values from -6 to 6
- out_grad: bfloat16 [8192, 4096], P('ctx', 'mp'), may hold values from -6 to 6
- neighbours: bfloat16 [128, 4, 128, 4096], P('ctx', None, None, 'mp'), may hold values from -6 to 6
- query_gain: float32 [128], replicated, may hold values from 0.6 to 2
- key_gain: float32 [128], replicated, may hold values from 0.6 to 2
- group_counts: int32 [128], replicated, may hold values from 1 to 4, as said below
- group_owners: int32 [128], replicated, may hold values from 0 to 63, as said below
Outputs:
- attended: bfloat16 [8192, 4096], P('ctx', 'mp')
- query_grad: bfloat16 [8192, 4096], P('ctx', 'mp')
- rows_grad: bfloat16 [8192, 4096], P('ctx', 'mp')
- gain_grads: float32 [2, 128], replicated
Inputs may be any that keep to these rules, and one draw needn't show every extreme that they name: `group_owners`: the owner of a group is the device that holds it or the next device along ctx (the last device hands to the first); every device hands exactly 1 of its 2 groups to the next device. `group_counts`: A group handed to the next device has at most 2 live neighbours; neighbour slots at or past a group's count are not read.
All inputs are finite; a program needn't handle non-finite values.
Results may differ from a plain program's by a relative error of at most 0.017.
Values may be sent and summed in bfloat16 or wider, within the bound.
A program may use at most 64 MiB of HBM per device.

v0:
```python
import math

import jax
import jax.numpy as jnp
from jax import lax
from jax.sharding import PartitionSpec as P

HEAD_SIZE = 128
KMAX = 4


EPSILON = 1e-06


def shifted(value, axis, steps):
    count = lax.axis_size(axis)
    pairs = [(source, (source + steps) % count) for source in range(count)]
    return lax.ppermute(value, axis, pairs)


def head_norm(value_rows):
    shaped = value_rows.astype(jnp.float32).reshape(
        value_rows.shape[:-1] + (value_rows.shape[-1] // HEAD_SIZE, HEAD_SIZE)
    )
    factor = lax.rsqrt(jnp.mean(shaped * shaped, axis=-1, keepdims=True) + EPSILON)
    return shaped * factor


def encode(neighbour_block, group_rows, query_gain, key_gain):
    slot_total, nbr_length, columns = neighbour_block.shape
    flattened = neighbour_block.reshape(slot_total * nbr_length, columns)
    encoder_query_rows = (head_norm(flattened) * query_gain).astype(jnp.bfloat16)
    encoder_key_rows = (head_norm(group_rows) * key_gain).astype(jnp.bfloat16)
    score_matrix = jnp.einsum(
        "yvo,jvo->vyj", encoder_key_rows, encoder_query_rows, preferred_element_type=jnp.float32
    ) / math.sqrt(HEAD_SIZE)
    powered = jnp.exp(score_matrix)
    softmax_weight = (powered / jnp.sum(powered, axis=1, keepdims=True)).astype(jnp.bfloat16)
    value_rows = group_rows.reshape(group_rows.shape[0], columns // HEAD_SIZE, HEAD_SIZE)
    weighted_value_mix = jnp.einsum(
        "rgq,gre->qre", softmax_weight, value_rows, preferred_element_type=jnp.float32
    )
    encoded = flattened.astype(jnp.float32) + weighted_value_mix.reshape(
        slot_total * nbr_length, columns
    )
    return encoded.astype(jnp.bfloat16).reshape(slot_total, nbr_length, columns)


def attend(query_rows, encoded, live_count):
    slot_total, nbr_length, columns = encoded.shape
    flattened = encoded.reshape(slot_total * nbr_length, columns)
    decoder_query_rows = head_norm(query_rows).astype(jnp.bfloat16)
    decoder_key_rows = head_norm(flattened).astype(jnp.bfloat16)
    score_matrix = jnp.einsum(
        "ybx,tbx->byt", decoder_query_rows, decoder_key_rows, preferred_element_type=jnp.float32
    ) / math.sqrt(HEAD_SIZE)
    live_keys = jnp.arange(slot_total * nbr_length, dtype=jnp.int32) // nbr_length < live_count
    powered = jnp.where(live_keys, jnp.exp(score_matrix), 0.0)
    softmax_weight = (powered / jnp.sum(powered, axis=-1, keepdims=True)).astype(jnp.bfloat16)
    value_rows = flattened.reshape(slot_total * nbr_length, columns // HEAD_SIZE, HEAD_SIZE)
    attention_output = jnp.einsum(
        "tuf,ftz->utz", softmax_weight, value_rows, preferred_element_type=jnp.float32
    )
    return attention_output.reshape(query_rows.shape[0], columns).astype(jnp.bfloat16)


def batch_encode(neighbours, slot_rows, query_gain, key_gain):
    return jax.vmap(encode, in_axes=(0, 0, None, None))(neighbours, slot_rows, query_gain, key_gain)


def batch_attend(query_blocks, encoded, live_counts):
    return jax.vmap(attend)(query_blocks, encoded, live_counts)


def listed(selected, how_many):
    return jnp.nonzero(selected, size=how_many)[0].astype(jnp.int32)


def pad_slots(block):
    return jnp.pad(block, ((0, 0), (0, KMAX - block.shape[1]), (0, 0), (0, 0)))


def per_device(
    hidden, queries, out_grad, neighbours, query_gain, key_gain, group_counts, group_owners
):
    here_index = lax.axis_index("ctx")
    groups = neighbours.shape[0]
    sent_count = groups // 2
    columns = hidden.shape[1]
    row_blocks = hidden.reshape(groups, -1, columns)
    query_blocks = queries.reshape(groups, -1, columns)
    grad_blocks = out_grad.reshape(groups, -1, columns)
    own_owner = lax.dynamic_slice_in_dim(group_owners, here_index * groups, groups)
    own_count = lax.dynamic_slice_in_dim(group_counts, here_index * groups, groups)
    handed = own_owner != here_index
    handed_list = listed(handed, sent_count)
    kept_list = listed(jnp.logical_not(handed), groups - sent_count)
    placing = jnp.concatenate([handed_list, kept_list])
    restore = jnp.zeros((groups,), jnp.int32).at[placing].set(jnp.arange(groups, dtype=jnp.int32))
    outgoing = jnp.take(row_blocks, handed_list, axis=0)[None]
    arrived = shifted(outgoing, "ctx", 1)
    slot_rows = jnp.concatenate([arrived[0], jnp.take(row_blocks, kept_list, axis=0)])
    encoded, encode_back = jax.vjp(
        lambda rows_in, gain_q, gain_k: batch_encode(neighbours, rows_in, gain_q, gain_k),
        slot_rows,
        query_gain,
        key_gain,
    )
    returned = encoded[:sent_count]
    came_back = shifted(returned, "ctx", -1)
    dec_encoded = jnp.take(
        jnp.concatenate([pad_slots(came_back), encoded[sent_count:]]), restore, axis=0
    )
    attended, decoder_back = jax.vjp(
        lambda query_in, encoded_in: batch_attend(query_in, encoded_in, own_count),
        query_blocks,
        dec_encoded,
    )
    grad_queries, grad_encoded = decoder_back(grad_blocks)
    handed_grad = jnp.take(grad_encoded, handed_list, axis=0)
    arrived_grad = shifted(handed_grad, "ctx", 1)
    slot_grad = jnp.concatenate(
        [pad_slots(arrived_grad), jnp.take(grad_encoded, kept_list, axis=0)]
    )
    grad_slot_rows, grad_gain_q, grad_gain_k = encode_back(slot_grad)
    returned_grad = grad_slot_rows[:sent_count][None]
    back_grad = shifted(returned_grad, "ctx", -1)
    grad_rows = jnp.take(
        jnp.concatenate([back_grad[0], grad_slot_rows[sent_count:]]), restore, axis=0
    )
    gain_grads = lax.psum(jnp.stack([grad_gain_q, grad_gain_k]), ("ctx", "mp"))
    return (
        attended.reshape(-1, columns),
        grad_queries.reshape(-1, columns),
        grad_rows.reshape(-1, columns),
        gain_grads,
    )


def solution(mesh):
    in_specs = (
        P("ctx", "mp"),
        P("ctx", "mp"),
        P("ctx", "mp"),
        P("ctx", None, None, "mp"),
        P(),
        P(),
        P(),
        P(),
    )
    out_specs = (P("ctx", "mp"), P("ctx", "mp"), P("ctx", "mp"), P())
    return jax.shard_map(
        per_device, mesh=mesh, in_specs=in_specs, out_specs=out_specs, check_vma=False
    )
```

profile of v0, /device:TPU:1, one launch (start us, length us, event | category | flops | bytes accessed | tf_op | source)
XLA Modules:
  0.0 201.1 jit_solution(321857917722629770)
XLA Ops:
  0.7 0.9 fusion.81
  1.5 0.6 fusion.82
  2.5 1.6 scatter_fusion.1
  6.7 1.6 scatter_fusion
  11.0 3.1 %collective-permute-start = (bf16[1,1,64,1024]{3,2,1,0:T(8,128)(2,1)S(1)}, bf16[1,1,64,1024]{3,2,1,0:T(8,128)(2,1)S(1)}, u32[]{:S(2)}, u32[]{:S(2)}) collective-permute-start(bf16[1,1,64,1024]{3,2,1,0:T(8,128)(2,1)S(1)} %get-tuple-element.41), channel_id=1, source_target_pairs={{0,4},{4,8},{8,12},{12,16},{16,20},{20,24},{24,28},{28,32},{32,36}... | collective-permute-start | bytes 393224 | tf_op jit(solution)/shard_map/ppermute | solution.py:18
  14.1 2.4 %convert_element_type.196 = f32[2,4,128,1024]{3,2,1,0:T(8,128)} convert(bf16[2,4,128,1024]{3,2,1,0:T(8,128)(2,1)S(1)} %copy-done.6) | non-fusion elementwise | flops 1048576 | bytes 6291456 | tf_op jit(solution)/shard_map/jvp(vmap())/convert_element_type | solution.py:43
  16.5 5.4 %copy.102 = f32[2,512,1024]{1,2,0:T(8,128)} copy(f32[2,512,1024]{2,1,0:T(8,128)} %bitcast.162) | data formatting | bytes 8388608 | tf_op jit(solution)/shard_map/jvp(vmap())/convert_element_type | solution.py:43
  21.9 3.2 %copy.124 = f32[128,8,8,128]{3,2,1,0:T(8,128)S(1)} copy(f32[128,8,8,128]{3,1,2,0:T(8,128)} %bitcast.163) | data formatting | bytes 8388608
  25.1 1.9 copy-done
  27.0 1.1 multiply_reduce_fusion
  28.5 0.6 scatter_custom_fusion.2
  29.8 4.0 %fusion.90 = (f32[2,8,512]{2,1,0:T(8,128)S(1)}, f32[2,8,64,512]{3,2,1,0:T(8,128)S(1)}) fusion(f32[2,512,8,128]{3,2,1,0:T(8,128)} %bitcast.159, f32[128]{0:T(128)S(1)} %copy-done.12, f32[2,512,8]{1,2,0:T(8,128)S(1)} %add_rsqrt_fusion, bf16[2,64,8,128]{3,1,2,0:T(8,128)(2,1)S(1)} %bitcast_dynamic-update-slice_fusion, f32[128]{0:T(128)S(1)} %copy-done.13, ...), kind=kOutput, calls=%fused_computation.146 | convolution fusion | flops 138928128 | bytes 6624256 | tf_op jit(solution)/shard_map/jvp(vmap(yvo,jvo->vyj))/dot_general | solution.py:34
  33.8 0.8 fusion.87
  34.6 1.4 copy-done.2
  36.0 1.1 fusion.4
  37.1 1.5 fusion.88
  38.6 2.3 %copy.103 = bf16[1,512,1024]{2,1,0:T(8,128)(2,1)} copy(bf16[1,512,1024]{1,2,0:T(8,128)(2,1)} %get-tuple-element.36) | data formatting | bytes 2097152 | tf_op jit(solution)/shard_map/slice | solution.py:109
  41.3 0.8 copy.127
  42.3 2.3 %copy.104 = bf16[1,512,1024]{2,1,0:T(8,128)(2,1)} copy(bf16[1,512,1024]{1,2,0:T(8,128)(2,1)} %get-tuple-element.37) | data formatting | bytes 2097152 | tf_op jit(solution)/shard_map/slice | solution.py:112
  44.6 10.8 %collective-permute-done.1 = bf16[1,4,128,1024]{3,2,1,0:T(8,128)(2,1)} collective-permute-done((bf16[1,4,128,1024]{3,2,1,0:T(8,128)(2,1)}, bf16[1,4,128,1024]{3,2,1,0:T(8,128)(2,1)}, u32[]{:S(2)}, u32[]{:S(2)}) %collective-permute-start.1) | collective-permute-done | bytes 1048608 | tf_op jit(solution)/shard_map/ppermute | solution.py:18
  55.5 3.1 %pad_maximum_fusion = bf16[2,4,128,1024]{3,2,1,0:T(8,128)(2,1)} fusion(bf16[1,4,128,1024]{3,2,1,0:T(8,128)(2,1)} %bitcast.179, bf16[1,4,128,1024]{3,2,1,0:T(8,128)(2,1)} %collective-permute-done.1), kind=kLoop, calls=%fused_computation.40 | loop fusion | flops 1048576 | bytes 4194304 | tf_op jit(solution)/shard_map/concatenate | solution.py:112
  58.5 3.6 %gather_fusion = bf16[2,4,128,1024]{3,2,1,0:T(8,128)(2,1)} fusion(bf16[2,4,128,1024]{3,2,1,0:T(8,128)(2,1)} %pad_maximum_fusion, s32[1024]{0:T(1024)S(1)} %pad_clamp_fusion), kind=kCustom, calls=%fused_computation | custom fusion | bytes 4194312 | tf_op jit(solution)/shard_map/jit(_take)/gather | solution.py:111
  62.2 2.2 %copy.125 = bf16[128,8,8,128]{3,2,1,0:T(8,128)(2,1)S(1)} copy(bf16[128,8,8,128]{3,1,2,0:T(8,128)(2,1)} %bitcast.172) | data formatting | bytes 4194304
  64.4 1.2 fusion.1
  65.6 2.0 %fusion.32 = (f32[2,8,64]{2,1,0:T(8,128)S(1)}, f32[2,8,64,512]{3,2,1,0:T(8,128)S(1)}) fusion(pred[2,512]{1,0:T(4,128)(4,1)S(1)} %broadcast_compare_fusion, f32[2,512,8]{1,2,0:T(8,128)S(1)} %fusion.68, bf16[2,512,8,128]{3,2,1,0:T(8,128)(2,1)S(1)} %bitcast.165, pred[2]{0:T(512)(128)(4,1)S(1)} %compare_and_fusion, f32[2,64,8,128]{3,2,1,0:T(8,128)S(1)} %bitcast.175, ...), kind=kOutput, calls=%fused_computation.57 | convolution fusion | flops 140246016 | bytes 4760578 | tf_op jit(solution)/shard_map/jvp(vmap(ybx,tbx->byt))/dot_general | solution.py:54
  67.7 1.0 fusion.47
  68.9 0.8 copy.187
  69.6 1.3 fusion.13
  71.0 2.6 %fusion.3 = (f32[2,512,8]{1,2,0:T(8,128)S(1)}, bf16[2,8,512,128]{3,2,1,0:T(8,128)(2,1)S(1)}) fusion(bf16[2,512,8,128]{3,2,1,0:T(8,128)(2,1)S(1)} %bitcast.168, pred[2]{0:T(512)(128)(4,1)S(1)} %compare_and_fusion, f32[2,64,8,128]{3,2,1,0:T(8,128)S(1)} %bitcast.176, f32[2,64,8]{1,2,0:T(8,128)S(1)} %fusion.70, ...), kind=kOutput, calls=%fused_computation.13 | convolution fusion | flops 144433152 | bytes 7910402 | tf_op jit(solution)/shard_map/transpose(jvp(vmap(ybx,tbx->byt)))/dot_general | solution.py:54
  73.6 4.2 %fusion.19 = bf16[2,512,8,128]{3,1,2,0:T(8,128)(2,1)S(1)} fusion(bf16[2,8,512,128]{3,2,1,0:T(8,128)(2,1)S(1)} %get-tuple-element.51, f32[2,512,8]{1,2,0:T(8,128)S(1)} %multiply_multiply_fusion, f32[2,512,8]{1,2,0:T(8,128)S(1)} %fusion.68, bf16[2,64,8,128]{3,2,1,0:T(8,128)(2,1)S(1)} %bitcast.190, f32[2,8,64,512]{3,2,1,0:T(8,128)S(1)} %get-tuple-element.45, ...), kind=kOutput, calls=%fused_computation.39 | convolution fusion | flops 146800640 | bytes 8721410 | tf_op jit(solution)/shard_map/transpose(jvp(vmap(tuf,ftz->utz)))/dot_general | solution.py:61
  77.8 2.6 %copy.114 = bf16[2,512,8,128]{3,2,1,0:T(8,128)(2,1)} copy(bf16[2,512,8,128]{3,1,2,0:T(8,128)(2,1)S(1)} %fusion.19) | data formatting | bytes 4194304 | tf_op jit(solution)/shard_map/transpose(jvp(vmap()))/add_any | solution.py:22
  80.4 4.2 %add_any.45 = bf16[2,4,128,1024]{3,2,1,0:T(8,128)(2,1)} reshape(bf16[2,512,8,128]{3,2,1,0:T(8,128)(2,1)} %copy.114) | data formatting | bytes 4194304 | tf_op jit(solution)/shard_map/transpose(jvp(vmap()))/add_any | solution.py:22
  84.6 1.9 dynamic-slice_select_fusion.1
  86.9 0.6 copy-done.16
  87.5 4.0 %multiply_reduce_fusion.1 = (f32[2,64,8]{1,2,0:T(8,128)S(1)}, f32[2,64,8,128]{3,1,2,0:T(8,128)S(1)}) fusion(f32[2,64,8,128]{3,2,1,0:T(8,128)S(1)} %bitcast.177, f32[2,512,8]{1,2,0:T(8,128)S(1)} %fusion.68, bf16[2,512,8,128]{3,2,1,0:T(8,128)(2,1)S(1)} %bitcast.170, pred[2]{0:T(512)(128)(4,1)S(1)} %compare_and_fusion, bf16[2,8,512,64]{2,3,1,0:T(8,128)(2,1)} %copy-done.17, ...), kind=kOutput, calls=%fused_computation.86 | convolution fusion | flops 142605312 | bytes 6337538 | tf_op jit(solution)/shard_map/transpose(jvp(vmap(ybx,tbx->byt)))/dot_general | solution.py:54
  92.0 0.8 copy.186
  92.8 5.8 %collective-permute-done.2 = bf16[1,4,128,1024]{3,2,1,0:T(8,128)(2,1)S(1)} collective-permute-done((bf16[1,4,128,1024]{3,2,1,0:T(8,128)(2,1)S(1)}, bf16[1,4,128,1024]{3,2,1,0:T(8,128)(2,1)S(1)}, u32[]{:S(2)}, u32[]{:S(2)}) %collective-permute-start.2) | collective-permute-done | bytes 1048608 | tf_op jit(solution)/shard_map/ppermute | solution.py:18
  98.8 2.0 copy.129
  100.7 4.4 %copy.119 = bf16[2,512,8,128]{1,3,2,0:T(8,128)(2,1)} copy(bf16[2,512,8,128]{3,2,1,0:T(8,128)(2,1)} %bitcast.173) | data formatting | bytes 4194304 | tf_op jit(solution)/shard_map/transpose(jvp(vmap()))/reshape | solution.py:43
  105.1 2.2 %fusion.18 = (f32[2,8,512]{2,1,0:T(8,128)S(1)}, bf16[2,8,64,512]{3,2,1,0:T(8,128)(2,1)S(1)}) fusion(f32[2,8,64,512]{3,2,1,0:T(8,128)S(1)} %get-tuple-element.43, f32[2,8,512]{2,1,0:T(8,128)S(1)} %multiply_divide_fusion, bf16[2,64,8,128]{3,1,2,0:T(8,128)(2,1)S(1)} %bitcast_dynamic-update-slice_fusion, bf16[2,512,8,128]{1,3,2,0:T(8,128)(2,1)} %copy.119), kind=kOutput, calls=%fused_computation.38 | convolution fusion | flops 136830976 | bytes 5570560 | tf_op jit(solution)/shard_map/transpose(jvp(vmap(rgq,gre->qre)))/dot_general | solution.py:40
  107.4 0.5 copy-done.1
  108.0 2.1 %fusion.57 = (f32[128]{0:T(128)S(1)}, f32[2,64,8]{1,2,0:T(8,128)S(1)}, f32[2,64,8,128]{3,1,2,0:T(8,128)S(1)}) fusion(bf16[2,64,8,128]{3,1,2,0:T(8,128)(2,1)S(1)} %bitcast_dynamic-update-slice_fusion, f32[2,64,8]{1,2,0:T(8,128)S(1)} %fusion.69, f32[128]{0:T(128)S(1)} %copy-done.13, f32[2,512,8,128]{3,2,1,0:T(8,128)S(1)} %bitcast.161, f32[128]{0:T(128)S(1)} %copy-done.12, ...), kind=kOutput, calls=%fused_computation.80 | convolution fusion | flops 141163392 | bytes 8234496 | tf_op jit(solution)/shard_map/transpose(jvp(vmap(yvo,jvo->vyj)))/dot_general | solution.py:34
  110.1 0.9 fusion.51
  111.2 10.4 %collective-permute-start.3 = (bf16[1,1,64,1024]{3,2,1,0:T(8,128)(2,1)S(1)}, bf16[1,1,64,1024]{3,2,1,0:T(8,128)(2,1)S(1)}, u32[]{:S(2)}, u32[]{:S(2)}) collective-permute-start(bf16[1,1,64,1024]{3,2,1,0:T(8,128)(2,1)S(1)} %broadcast_in_dim.117), channel_id=1, source_target_pairs={{0,252},{4,0},{8,4},{12,8},{16,12},{20,16},{24,20},{28,24},{32,28}... | collective-permute-start | bytes 393224 | tf_op jit(solution)/shard_map/ppermute | solution.py:18
  121.6 4.4 %fusion.5 = f32[128]{0:T(128)S(1)} fusion(f32[2,512,8,128]{3,2,1,0:T(8,128)} %bitcast.160, f32[2,512,8]{1,2,0:T(8,128)S(1)} %add_rsqrt_fusion, bf16[2,64,8,128]{3,1,2,0:T(8,128)(2,1)S(1)} %bitcast_dynamic-update-slice_fusion, f32[128]{0:T(128)S(1)} %copy-done.13, f32[2,64,8]{1,2,0:T(8,128)S(1)} %fusion.69, f32[2,8,64,512]{3,2,1,0:T(8,128)S(1)} %get-tuple-element.43, ...), kind=kOutput, calls=%fused_computation.17 | convolution fusion | flops 142606208 | bytes 7705600 | tf_op jit(solution)/shard_map/transpose(jvp(vmap(yvo,jvo->vyj)))/dot_general | solution.py:34
  126.1 73.7 %psum.7 = f32[2,128]{1,0:T(2,128)} all-reduce(f32[2,128]{1,0:T(2,128)S(1)} %pad_maximum_fusion.3), channel_id=1, replica_groups=mesh['ctx'=64,'mp'=4] {'ctx','mp'}, use_global_device_ids=true, to_apply=%region_20.23 | all-reduce | flops 256 | bytes 2048 | tf_op jit(solution)/shard_map/psum | solution.py:131
  199.8 0.6 gather_fusion.1
  200.3 0.8 bitcast_select_fusion
  (82 shorter events, 3.5 us)
Async XLA Ops:
  0.6 10.3 %copy-start.9 = (bf16[128,1024]{1,0:T(8,128)(2,1)S(1)}, bf16[128,1024]{1,0:T(8,128)(2,1)}, u32[]{:S(2)}) copy-start(bf16[128,1024]{1,0:T(8,128)(2,1)} %param.12) | copy-start | bytes 786436
  0.6 13.5 %copy-start.6 = (bf16[2,4,128,1024]{3,2,1,0:T(8,128)(2,1)S(1)}, bf16[2,4,128,1024]{3,2,1,0:T(8,128)(2,1)}, u32[]{:S(2)}) copy-start(bf16[2,4,128,1024]{3,2,1,0:T(8,128)(2,1)} %param.15) | copy-start | bytes 6291460
  11.0 18.5 %collective-permute-start = (bf16[1,1,64,1024]{3,2,1,0:T(8,128)(2,1)S(1)}, bf16[1,1,64,1024]{3,2,1,0:T(8,128)(2,1)S(1)}, u32[]{:S(2)}, u32[]{:S(2)}) collective-permute-start(bf16[1,1,64,1024]{3,2,1,0:T(8,128)(2,1)S(1)} %get-tuple-element.41), channel_id=1, source_target_pairs={{0,4},{4,8},{8,12},{12,16},{16,20},{20,24},{24,28},{28,32},{32,36}... | collective-permute-start | bytes 393224 | tf_op jit(solution)/shard_map/ppermute | solution.py:18
  25.1 1.9 copy-start
  27.0 2.1 %copy-start.8 = (bf16[128,1024]{1,0:T(8,128)(2,1)S(1)}, bf16[128,1024]{1,0:T(8,128)(2,1)}, u32[]{:S(2)}) copy-start(bf16[128,1024]{1,0:T(8,128)(2,1)} %param.13) | copy-start | bytes 786436
  28.2 1.6 copy-start.12
  28.2 1.6 copy-start.13
  33.8 2.2 %copy-start.2 = (f32[2,512,1024]{1,2,0:T(8,128)S(1)}, f32[2,512,1024]{1,2,0:T(8,128)}, u32[]{:S(2)}) copy-start(f32[2,512,1024]{1,2,0:T(8,128)} %copy.102) | copy-start | bytes 12582916
  38.6 2.6 %copy-start.14 = (s32[128]{0:T(128)S(1)}, s32[128]{0:T(128)}, u32[]{:S(2)}) copy-start(s32[128]{0:T(128)} %param.18) | copy-start | bytes 1540
  38.6 2.7 %copy-start.10 = (bf16[128,1024]{1,0:T(8,128)(2,1)S(1)}, bf16[128,1024]{1,0:T(8,128)(2,1)}, u32[]{:S(2)}) copy-start(bf16[128,1024]{1,0:T(8,128)(2,1)} %param.14) | copy-start | bytes 786436
  40.9 14.5 %collective-permute-start.1 = (bf16[1,4,128,1024]{3,2,1,0:T(8,128)(2,1)}, bf16[1,4,128,1024]{3,2,1,0:T(8,128)(2,1)}, u32[]{:S(2)}, u32[]{:S(2)}) collective-permute-start(bf16[1,4,128,1024]{3,2,1,0:T(8,128)(2,1)} %bitcast.180), channel_id=1, source_target_pairs={{0,252},{4,0},{8,4},{12,8},{16,12},{20,16},{24,20},{28,24},{32,28}... | collective-permute-start | bytes 3145736 | tf_op jit(solution)/shard_map/ppermute | solution.py:18
  64.4 9.2 %copy-start.3 = (bf16[128,8,8,128]{3,2,1,0:T(8,128)(2,1)}, bf16[128,8,8,128]{3,2,1,0:T(8,128)(2,1)S(1)}, u32[]{:S(2)}) copy-start(bf16[128,8,8,128]{3,2,1,0:T(8,128)(2,1)S(1)} %copy.125) | copy-start | bytes 6291460
  67.7 5.9 %copy-start.15 = (f32[2,8,64,512]{3,2,1,0:T(8,128)}, f32[2,8,64,512]{3,2,1,0:T(8,128)S(1)}, u32[]{:S(2)}) copy-start(f32[2,8,64,512]{3,2,1,0:T(8,128)S(1)} %get-tuple-element.45) | copy-start | bytes 6291460
  67.7 2.0 copy-start.11
  70.9 2.6 %copy-start.17 = (bf16[2,8,512,64]{2,3,1,0:T(8,128)(2,1)}, bf16[2,8,512,64]{2,3,1,0:T(8,128)(2,1)S(1)}, u32[]{:S(2)}) copy-start(bf16[2,8,512,64]{2,3,1,0:T(8,128)(2,1)S(1)} %get-tuple-element.47) | copy-start | bytes 3145732
  84.6 2.2 %copy-start.4 = (bf16[128,8,8,128]{3,2,1,0:T(8,128)(2,1)S(1)}, bf16[128,8,8,128]{3,2,1,0:T(8,128)(2,1)}, u32[]{:S(2)}) copy-start(bf16[128,8,8,128]{3,2,1,0:T(8,128)(2,1)} %copy-done.3) | copy-start | bytes 6291460
  84.6 2.9 %copy-start.16 = (f32[2,8,64,512]{3,2,1,0:T(8,128)S(1)}, f32[2,8,64,512]{3,2,1,0:T(8,128)}, u32[]{:S(2)}) copy-start(f32[2,8,64,512]{3,2,1,0:T(8,128)} %copy-done.15) | copy-start | bytes 6291460
  86.5 12.0 %collective-permute-start.2 = (bf16[1,4,128,1024]{3,2,1,0:T(8,128)(2,1)S(1)}, bf16[1,4,128,1024]{3,2,1,0:T(8,128)(2,1)S(1)}, u32[]{:S(2)}, u32[]{:S(2)}) collective-permute-start(bf16[1,4,128,1024]{3,2,1,0:T(8,128)(2,1)S(1)} %get-tuple-element.34), channel_id=1, source_target_pairs={{0,4},{4,8},{8,12},{12,16},{16,20},{20,24},{24,28},{28,32},{32,36}... | collective-permute-start | bytes 3145736 | tf_op jit(solution)/shard_map/ppermute | solution.py:18
  105.1 2.8 %copy-start.1 = (f32[128,8,8,128]{3,2,1,0:T(8,128)S(1)}, f32[128,8,8,128]{3,2,1,0:T(8,128)}, u32[]{:S(2)}) copy-start(f32[128,8,8,128]{3,2,1,0:T(8,128)} %copy-done) | copy-start | bytes 12582916
  107.4 2.7 %copy-start.7 = (bf16[2,8,64,512]{3,2,1,0:T(8,128)(2,1)}, bf16[2,8,64,512]{3,2,1,0:T(8,128)(2,1)S(1)}, u32[]{:S(2)}) copy-start(bf16[2,8,64,512]{3,2,1,0:T(8,128)(2,1)S(1)} %get-tuple-element.53) | copy-start | bytes 3145732
  108.0 2.1 %copy-start.5 = (bf16[2,512,8,128]{1,3,2,0:T(8,128)(2,1)S(1)}, bf16[2,512,8,128]{1,3,2,0:T(8,128)(2,1)}, u32[]{:S(2)}) copy-start(bf16[2,512,8,128]{1,3,2,0:T(8,128)(2,1)} %copy.119) | copy-start | bytes 6291460
  111.2 88.5 %collective-permute-start.3 = (bf16[1,1,64,1024]{3,2,1,0:T(8,128)(2,1)S(1)}, bf16[1,1,64,1024]{3,2,1,0:T(8,128)(2,1)S(1)}, u32[]{:S(2)}, u32[]{:S(2)}) collective-permute-start(bf16[1,1,64,1024]{3,2,1,0:T(8,128)(2,1)S(1)} %broadcast_in_dim.117), channel_id=1, source_target_pairs={{0,252},{4,0},{8,4},{12,8},{16,12},{20,16},{24,20},{28,24},{32,28}... | collective-permute-start | bytes 393224 | tf_op jit(solution)/shard_map/ppermute | solution.py:18
where the time goes:
time: 202 us; the launch traced here: 201 us
  blocking collectives  73.7 us (36%)
  local copies, waits for them, and re-layouts  42.9 us (21%)
  matrix products  29.5 us (15%)
  other arithmetic  18.1 us (9%)
  waiting for transfers between devices  16.6 us (8%)
  starting transfers between devices  14 us (7%)
  between operations  6.38 us (3%)
    psum x1, blocking collectives, per_device(): gain_grads = lax.psum(jnp.stack([grad_gain_q, grad_gain_k]), ('ctx', 'mp'))  73.7 us
    ppermute x4, waiting for transfers between devices, shifted(): return lax.ppermute(value, axis, pairs)  16.6 us
    unnamed x45, local copies, waits for them, and re-layouts  14.4 us
    ppermute x4, starting transfers between devices, shifted(): return lax.ppermute(value, axis, pairs)  14 us
    dot_general x3, matrix products, encode(): jnp.einsum('yvo,jvo->vyj', encoder_key_rows, encoder_query_rows, preferre...  10.5 us
    dot_general x3, matrix products, attend(): jnp.einsum('ybx,tbx->byt', decoder_query_rows, decoder_key_rows, preferre...  8.63 us
    add_any x2, local copies, waits for them, and re-layouts, head_norm(): value_rows.astype(jnp.float32)  6.85 us
    dot_general x3, matrix products, attend(): jnp.einsum('tuf,ftz->utz', softmax_weight, value_rows, preferred_element_...  6.45 us
  transfers between devices with their start and end apart: 4, of which 2 were waited for; matrix products, arithmetic and copies ran while one was open for 13% of the time, Pallas kernels for 0%

commit v1 on v0

v1 whole, which is shorter than its diff:
```python
import functools
import math

import jax
import jax.numpy as jnp
from jax import lax
from jax.experimental import pallas as pl
from jax.experimental.pallas import tpu as pltpu
from jax.sharding import PartitionSpec as P

HEAD = 128
ROWS = 64
NBR = 128
SLOTS = 4
SENT_SLOTS = 2
EPSILON = 1e-06
SCALE = 1.0 / math.sqrt(HEAD)
LOG2E = math.log2(math.e)
MESH = pl.DeviceIdType.MESH
VMEM_LIMIT = 64 * 1024 * 1024 - 256 * 1024
BF16 = jnp.bfloat16
F32 = jnp.float32


def mm(a, b):
    return lax.dot_general(a, b, (((1,), (0,)), ((), ())), preferred_element_type=F32)


def mm_nt(a, b):
    return lax.dot_general(a, b, (((1,), (1,)), ((), ())), preferred_element_type=F32)


def mm_tn(a, b):
    return lax.dot_general(a, b, (((0,), (0,)), ((), ())), preferred_element_type=F32)


def row_norm(value):
    wide = value.astype(F32)
    factor = lax.rsqrt(jnp.mean(wide * wide, axis=1, keepdims=True) + EPSILON)
    return wide * factor, factor


def unit(x, h, q, g, gain, live, result):
    hn, rh = row_norm(h)
    qn, rq = row_norm(q)
    ek = (hn * gain).astype(BF16)
    qg = jnp.concatenate([qn.astype(BF16), g], axis=0)
    xt = jnp.transpose(x)
    xtf = xt.astype(F32)
    rx = lax.rsqrt(jnp.mean(xtf * xtf, axis=0, keepdims=True) + EPSILON)
    yield
    s = mm(ek, xt)
    yield
    p = jnp.exp2(s * (rx * (SCALE * LOG2E)))
    w = p * (1.0 / jnp.sum(p, axis=0, keepdims=True))
    wb = w.astype(BF16)
    yield
    e = xtf + mm_tn(h, wb)
    eb = e.astype(BF16)
    ef = eb.astype(F32)
    re = lax.rsqrt(jnp.mean(ef * ef, axis=0, keepdims=True) + EPSILON)
    yield
    both = mm(qg, eb)
    yield
    t, da = both[:ROWS], both[ROWS:]
    p = jnp.exp2(t * (re * (SCALE * LOG2E))) * live
    a = p * (1.0 / jnp.sum(p, axis=1, keepdims=True))
    z = a * (da - jnp.sum(a * da, axis=1, keepdims=True))
    dt = z * (re * SCALE)
    c = jnp.sum(dt * t, axis=0, keepdims=True) * (re * re * (1.0 / HEAD))
    ta = jnp.concatenate([dt.astype(BF16), a.astype(BF16)], axis=0)
    yield
    deb = (mm_tn(qg, ta) - ef * c).astype(BF16)
    yield
    dw = mm(h, deb)
    dqo = mm_nt(ta, eb)
    yield
    ds = w * (dw - jnp.sum(w * dw, axis=0, keepdims=True))
    ux = mm((ds * (rx * SCALE)).astype(BF16), x)
    dh = mm_nt(wb, deb)
    yield
    dqn = dqo[:ROWS]
    dq = rq * (dqn - qn * jnp.mean(dqn * qn, axis=1, keepdims=True))
    dhn = ux * gain
    dh = dh + rh * (dhn - hn * jnp.mean(dhn * hn, axis=1, keepdims=True))
    v = jnp.sum(ux * hn, axis=0, keepdims=True)
    result.append((dqo[ROWS:].astype(BF16), dq.astype(BF16), dh.astype(BF16), v))


def lockstep(makers):
    results = [[] for _ in makers]
    running = [make(result) for make, result in zip(makers, results)]
    while running:
        running = [r for r in running if next(r, "end") != "end"]
    return [r[0] for r in results]


def phase_near(c, m):
    pos = c % 16
    return pos, 16, lambda j: (c - pos + (pos + j) % 16, m)


def phase_far(c, m):
    pos = (c // 16) * 4 + m
    return pos, 16, lambda j: ((c % 16) + 16 * (((pos + j) % 16) // 4), (pos + j) % 4)


def main_kernel(
    heads, counts, owners, hidden, queries, out_grad, nbrs, gq, gk,
    att_out, dq_out, dh_out, v_out,
    h_buf, q_buf, g_buf, kept_buf, sent_buf, att, dq, dh, v_acc, got_near, got_far,
    in_sem, kept_sem, out_sem, send_sem, recv_sem, sum_send, sum_recv,
):
    c = lax.axis_index("ctx")
    m = lax.axis_index("mp")
    n = lax.axis_size("ctx")
    following, preceding = (c + 1) % n, (c + n - 1) % n
    phases = [phase_near(c, m), phase_far(c, m)]
    barrier = pltpu.get_barrier_semaphore()
    greeted = 0
    for d in (following, preceding):
        pl.semaphore_signal(barrier, inc=1, device_id=(d, m), device_id_type=MESH)
        greeted += 1
    for _, size, partner in phases:
        for j in range(1, size):
            pl.semaphore_signal(barrier, inc=1, device_id=partner(j), device_id_type=MESH)
            greeted += 1
    loads = [
        pltpu.make_async_copy(src, dst, in_sem.at[i])
        for i, (src, dst) in enumerate(((hidden, h_buf), (queries, q_buf), (out_grad, g_buf)))
    ]
    for load in loads:
        load.start()
    columns = heads * HEAD
    half = heads // 2
    width = half * HEAD
    kept_loads = [
        pltpu.make_async_copy(
            nbrs.at[1, :, :, pl.ds(i * width, width)], kept_buf.at[:, :, pl.ds(i * width, width)], kept_sem.at[i]
        )
        for i in range(2)
    ]
    for load in kept_loads:
        load.start()
    pl.semaphore_wait(barrier, greeted)
    sends = []
    for i in range(heads):
        cols = pl.ds(i * HEAD, HEAD)
        send = pltpu.make_async_remote_copy(
            src_ref=nbrs.at[0, pl.ds(0, SENT_SLOTS), :, cols],
            dst_ref=sent_buf.at[:, :, cols],
            send_sem=send_sem.at[i],
            recv_sem=recv_sem.at[i],
            device_id=(preceding, m),
            device_id_type=MESH,
        )
        send.start()
        sends.append(send)
    for load in loads:
        load.wait()
    for load in kept_loads:
        load.wait()
    gain = gq[...] * gk[...]
    first_kept = jnp.full((ROWS, columns), owners[2 * c], jnp.int32) == c
    lanes = lax.broadcasted_iota(jnp.int32, (1, SLOTS * NBR), 1)
    first_kept_lanes = jnp.full(lanes.shape, owners[2 * c], jnp.int32) == c
    first = jnp.full(lanes.shape, counts[2 * c] * NBR, jnp.int32)
    second = jnp.full(lanes.shape, counts[2 * c + 1] * NBR, jnp.int32)
    live = jnp.where(lanes < jnp.where(first_kept_lanes, first, second), 1.0, 0.0)
    live_sent = jnp.where(lanes < jnp.where(first_kept_lanes, second, first), 1.0, 0.0)
    live_sent = live_sent[:, : SENT_SLOTS * NBR]
    for buf in (h_buf, q_buf, g_buf):
        top, bottom = buf[:ROWS], buf[ROWS:]
        buf[:ROWS] = jnp.where(first_kept, top, bottom)
        buf[ROWS:] = jnp.where(first_kept, bottom, top)
    kept_rows, handed_rows = pl.ds(0, ROWS), pl.ds(ROWS, ROWS)
    v_acc[...] = jnp.zeros_like(v_acc)

    def work(head_list, slot, rows, nbr_buf, mask):
        makers = []
        for i in head_list:
            cols = pl.ds(pl.multiple_of(i * HEAD, HEAD), HEAD)
            x = nbr_buf[:, :, cols].reshape(-1, HEAD)
            makers.append(
                functools.partial(
                    unit, x, h_buf[rows, cols], q_buf[rows, cols], g_buf[rows, cols], gain, mask
                )
            )
        total = v_acc[...]
        for i, (o, one_dq, one_dh, v) in zip(head_list, lockstep(makers)):
            cols = pl.ds(pl.multiple_of(i * HEAD, HEAD), HEAD)
            att[slot, :, cols] = o
            dq[slot, :, cols] = one_dq
            dh[slot, :, cols] = one_dh
            total = total + v
        v_acc[...] = total

    def kept_step(i, carry):
        work([2 * i, 2 * i + 1], 0, kept_rows, kept_buf, live)
        return carry

    lax.fori_loop(0, heads // 2, kept_step, 0)
    for i in range(0, heads, 2):
        sends[i].wait_recv()
        sends[i + 1].wait_recv()
        work([i, i + 1], 1, handed_rows, sent_buf, live_sent)

    for p, (pos, size, partner) in enumerate(phases):
        got = (got_near, got_far)[p]
        for j in range(1, size):
            pltpu.make_async_remote_copy(
                src_ref=v_acc, dst_ref=got.at[pos], send_sem=sum_send.at[p], recv_sem=sum_recv.at[p],
                device_id=partner(j), device_id_type=MESH,
            ).start()
        got[pos] = v_acc[...]
        if p == 0:
            for buf, slots in ((h_buf, att), (q_buf, dq), (g_buf, dh)):
                buf[:ROWS] = jnp.where(first_kept, slots[0], slots[1])
                buf[ROWS:] = jnp.where(first_kept, slots[1], slots[0])
            stores = [
                pltpu.make_async_copy(src, dst, out_sem.at[i])
                for i, (src, dst) in enumerate(((h_buf, att_out), (q_buf, dq_out), (g_buf, dh_out)))
            ]
            for store in stores:
                store.start()
        sent = got.at[pl.ds(0, size - 1)]
        pltpu.make_async_copy(sent, sent, sum_send.at[p]).wait()
        pltpu.make_async_copy(sent, sent, sum_recv.at[p]).wait()
        v_acc[...] = jnp.sum(got[...], axis=0)
    v_out[...] = v_acc[...]
    for store in stores:
        store.wait()
    for send in sends:
        send.wait_send()


def last_kernel(att, dq, dh, v, gq, gk, att_out, dq_out, dh_out, gains_out, buf, in_sem, out_sem):
    loads = [
        pltpu.make_async_copy(src, buf.at[i], in_sem.at[i]) for i, src in enumerate((att, dq, dh))
    ]
    stores = [
        pltpu.make_async_copy(buf.at[i], dst, out_sem.at[i])
        for i, dst in enumerate((att_out, dq_out, dh_out))
    ]
    for load in loads:
        load.start()
    gains_out[0:1, :] = v[...] * gk[...]
    gains_out[1:2, :] = v[...] * gq[...]
    for load, store in zip(loads, stores):
        load.wait()
        store.start()
    for store in stores:
        store.wait()


def per_device(hidden, queries, out_grad, nbrs, query_gain, key_gain, counts, owners):
    rows, columns = hidden.shape
    heads = columns // HEAD
    block = jax.ShapeDtypeStruct((rows, columns), BF16)
    smem = pl.BlockSpec(memory_space=pltpu.SMEM)
    vmem = pl.BlockSpec(memory_space=pltpu.VMEM)
    hbm = pl.BlockSpec(memory_space=pl.ANY)
    dma = pltpu.SemaphoreType.DMA
    gq, gk = query_gain[None], key_gain[None]
    att, dq, dh, v = pl.pallas_call(
        functools.partial(main_kernel, heads),
        out_shape=[block, block, block, jax.ShapeDtypeStruct((1, HEAD), F32)],
        in_specs=[smem, smem, hbm, hbm, hbm, hbm, vmem, vmem],
        out_specs=[hbm, hbm, hbm, vmem],
        scratch_shapes=[
            *[pltpu.VMEM((rows, columns), BF16)] * 3,
            pltpu.VMEM((SLOTS, NBR, columns), BF16),
            pltpu.VMEM((SENT_SLOTS, NBR, columns), BF16),
            *[pltpu.VMEM((2, ROWS, columns), BF16)] * 3,
            pltpu.VMEM((1, HEAD), F32),
            pltpu.VMEM((16, 1, HEAD), F32),
            pltpu.VMEM((16, 1, HEAD), F32),
            dma((3,)), dma((2,)), dma((3,)), dma((heads,)), dma((heads,)), dma((2,)), dma((2,)),
        ],
        compiler_params=pltpu.CompilerParams(
            collective_id=0, has_side_effects=True, vmem_limit_bytes=VMEM_LIMIT
        ),
    )(counts, owners, hidden, queries, out_grad, nbrs, gq, gk)
    return pl.pallas_call(
        last_kernel,
        out_shape=[block, block, block, jax.ShapeDtypeStruct((2, HEAD), F32)],
        in_specs=[hbm, hbm, hbm, vmem, vmem, vmem],
        out_specs=[hbm, hbm, hbm, vmem],
        scratch_shapes=[pltpu.VMEM((3, rows, columns), BF16), dma((3,)), dma((3,))],
        compiler_params=pltpu.CompilerParams(vmem_limit_bytes=VMEM_LIMIT),
    )(att, dq, dh, v, gq, gk)


def solution(mesh):
    in_specs = (
        P("ctx", "mp"),
        P("ctx", "mp"),
        P("ctx", "mp"),
        P("ctx", None, None, "mp"),
        P(),
        P(),
        P(),
        P(),
    )
    out_specs = (P("ctx", "mp"), P("ctx", "mp"), P("ctx", "mp"), P())
    return jax.shard_map(
        per_device, mesh=mesh, in_specs=in_specs, out_specs=out_specs, check_vma=False
    )
```

time: 202 us -> 34.6 us (0.17)
  blocking collectives: 73.7 us -> 0 us
  local copies, waits for them, and re-layouts: 42.9 us -> 0 us
  Pallas kernels: 0 us -> 33.8 us
  matrix products: 29.5 us -> 0 us
  other arithmetic: 18.1 us -> 0 us
  waiting for transfers between devices: 16.6 us -> 0 us
  starting transfers between devices: 14 us -> 0 us
  between operations: 6.38 us -> 0.64 us
    psum x1 -> x0, blocking collectives: 73.7 us -> none  [per_device(): gain_grads = lax.psum(jnp.stack([grad_gain_q, grad_gain_k]), ('ctx', 'mp'))]
    pallas_call x0 -> x2, Pallas kernels: none -> 33.8 us  [the longest x1 30.7 us: per_device(): pl.pallas_call(functools.partial(main_kernel, heads), out_shape=[block, b...]
    dot_general x12 -> x0, matrix products: 29.5 us -> none  [the longest x3 10.5 us: encode(): jnp.einsum('yvo,jvo->vyj', encoder_key_rows, encoder_query_rows, preferre...]
    ppermute x4 -> x0, waiting for transfers between devices: 16.6 us -> none  [shifted(): return lax.ppermute(value, axis, pairs)]
    unnamed x45 -> x0, local copies, waits for them, and re-layouts: 14.4 us -> none
    ppermute x4 -> x0, starting transfers between devices: 14 us -> none  [shifted(): return lax.ppermute(value, axis, pairs)]
    add_any x2 -> x0, local copies, waits for them, and re-layouts: 6.85 us -> none  [head_norm(): value_rows.astype(jnp.float32)]
    slice x6 -> x0, local copies, waits for them, and re-layouts: 6.22 us -> none  [the longest x2 3.79 us: per_device(): returned = encoded[:sent_count]]
  transfers between devices with their start and end apart: 4 -> 0, of which waited for: 2 -> 0; matrix products, arithmetic and copies ran while one was open for 13% -> 0% of each run, Pallas kernels for 0% -> 0%
where the time goes in v1:
time: 34.6 us; the launch traced here: 34.5 us
  Pallas kernels  33.8 us (98%)
  between operations  0.64 us (2%)
    pallas_call x1, Pallas kernels, per_device(): pl.pallas_call(functools.partial(main_kernel, heads), out_shape=[block, b...  30.7 us
    pallas_call x1, Pallas kernels, per_device(): pl.pallas_call(last_kernel, out_shape=[block, block, block, jax.ShapeDtyp...  3.12 us

profile of v1, /device:TPU:1, one launch (start us, length us, event | category | flops | bytes accessed | tf_op | source)
XLA Modules:
  0.0 34.5 jit_solution(8929548098798537764)
XLA Ops:
  0.6 30.7 %shard_map.111 = (bf16[128,1024]{1,0:T(8,128)(2,1)}, bf16[128,1024]{1,0:T(8,128)(2,1)}, bf16[128,1024]{1,0:T(8,128)(2,1)}, f32[1,128]{1,0:T(1,128)}) custom-call(s32[128]{0:T(128)} %counts.1, s32[128]{0:T(128)} %owners.1, bf16[128,1024]{1,0:T(8,128)(2,1)} %hidden.1, bf16[128,1024]{1,0:T(8,128)(2,1)} %queries.1, bf16[128,1024]{1,0:T(8,128)(2,1)} %out_grad.1, ...), custom_call_target="tpu_custom_call" | custom-call | tf_op jit(solution)/shard_map/pallas_call | solution.py:265
  31.4 3.1 %shard_map.112 = (bf16[128,1024]{1,0:T(8,128)(2,1)}, bf16[128,1024]{1,0:T(8,128)(2,1)}, bf16[128,1024]{1,0:T(8,128)(2,1)}, f32[2,128]{1,0:T(2,128)}) custom-call(bf16[128,1024]{1,0:T(8,128)(2,1)} %get-tuple-element.8.att, bf16[128,1024]{1,0:T(8,128)(2,1)} %get-tuple-element.9.dq, bf16[128,1024]{1,0:T(8,128)(2,1)} %get-tuple-element.10.dh, ...), custom_call_target="tpu_custom_call" | custom-call | tf_op jit(solution)/shard_map/pallas_call | solution.py:284

commit v2 on v1

v2 whole, which is shorter than its diff:
```python
import functools
import math

import jax
import jax.numpy as jnp
from jax import lax
from jax.experimental import pallas as pl
from jax.experimental.pallas import tpu as pltpu
from jax.sharding import PartitionSpec as P

HEAD = 128
ROWS = 64
NBR = 128
SLOTS = 4
SENT_SLOTS = 2
PAIR = 2 * HEAD
EPSILON = 1e-06
SCALE = 1.0 / math.sqrt(HEAD)
LOG2E = math.log2(math.e)
MESH = pl.DeviceIdType.MESH
VMEM_LIMIT = 63 * 1024 * 1024
BF16 = jnp.bfloat16
F32 = jnp.float32


def mm(a, b):
    return lax.dot_general(a, b, (((1,), (0,)), ((), ())), preferred_element_type=F32)


def mm_nt(a, b):
    return lax.dot_general(a, b, (((1,), (1,)), ((), ())), preferred_element_type=F32)


def mm_tn(a, b):
    return lax.dot_general(a, b, (((0,), (0,)), ((), ())), preferred_element_type=F32)


def row_norm(value):
    wide = value.astype(F32)
    factor = lax.rsqrt(jnp.mean(wide * wide, axis=1, keepdims=True) + EPSILON)
    return wide * factor, factor


def over_rows(value, row):
    k = row.shape[0]
    return (value.reshape(-1, k, value.shape[1]) * row[None]).reshape(value.shape)


def unit(x, h, q, g, gain, live, result):
    eye = (
        lax.broadcasted_iota(jnp.int32, (HEAD, HEAD), 0)
        == lax.broadcasted_iota(jnp.int32, (HEAD, HEAD), 1)
    ).astype(BF16)
    ones = jnp.ones((16, HEAD), BF16)
    root = math.sqrt(HEAD)
    xt = jnp.transpose(x)
    hf, qf = h.astype(F32), q.astype(F32)
    rh = lax.rsqrt(jnp.sum(hf * hf, axis=1, keepdims=True) + HEAD * EPSILON)
    rq = lax.rsqrt(jnp.sum(qf * qf, axis=1, keepdims=True) + HEAD * EPSILON)
    hn, qn = hf * rh, qf * rq
    ek = (hn * gain).astype(BF16)
    qg = jnp.concatenate([qn.astype(BF16), g], axis=0)
    rx = lax.rsqrt(mm(ones, xt * xt) + HEAD * EPSILON)
    yield
    s = mm(ek, xt)
    yield
    p = jnp.exp2(over_rows(s, rx[:8] * (root * LOG2E)))
    wb = (p * (1.0 / jnp.sum(p, axis=0, keepdims=True))).astype(BF16)
    yield
    eb = mm(jnp.concatenate([eye, jnp.transpose(h)], axis=1), jnp.concatenate([xt, wb], axis=0)).astype(BF16)
    yield
    both = mm(qg, eb)
    re = lax.rsqrt(mm(ones, eb * eb) + HEAD * EPSILON)
    yield
    t, da = both[:ROWS], both[ROWS:]
    p = jnp.exp2(over_rows(t, re[:8] * (root * LOG2E)))
    p = jnp.concatenate([p[:, :NBR], p[:, NBR:] * live[:, NBR:]], axis=1)
    inv = 1.0 / jnp.sum(p, axis=1, keepdims=True)
    shift = jnp.sum(p * da, axis=1, keepdims=True) * inv
    ab = (p * inv).astype(BF16)
    dt = over_rows(ab * (da - shift).astype(BF16), (re * root).astype(BF16))
    ta = jnp.concatenate([dt, ab], axis=0)
    yield
    c = mm(ones[:, :ROWS], dt * t.astype(BF16)) * (re * re)
    ec = over_rows(eb, (-c).astype(BF16))
    yield
    deb = mm(jnp.concatenate([jnp.transpose(qg), eye], axis=1), jnp.concatenate([ta, ec], axis=0)).astype(BF16)
    yield
    dw = mm(h, deb)
    yield
    dk = mm(ones[:, :ROWS], wb * dw.astype(BF16))
    ds = wb * (dw.reshape(-1, 8, dw.shape[1]) - dk[None, :8]).reshape(dw.shape).astype(BF16)
    yield
    ux = mm(over_rows(ds, (rx * root).astype(BF16)), x)
    yield
    u = ux * hn
    result.append(jnp.sum(u, axis=0, keepdims=True))
    yield "v"
    dqo = mm_nt(ta, eb)
    dh = mm_nt(wb, deb)
    yield
    dqn = dqo[:ROWS]
    dq = rq * (dqn - qn * jnp.sum(dqn * qn, axis=1, keepdims=True))
    dh = dh + rh * (ux * gain - hn * jnp.sum(u * gain, axis=1, keepdims=True))
    result.append((dqo[ROWS:].astype(BF16), dq.astype(BF16), dh.astype(BF16)))


def staggered(waiting, every, finish, later, at_once=1):
    waiting, running, tick = list(waiting), [], 0
    while waiting or running:
        if tick % every == 0:
            running, waiting = running + waiting[:at_once], waiting[at_once:]
        still = []
        for number, steps in running:
            if not hasattr(steps, "send"):
                steps = steps()
            mark = next(steps, "end")
            if mark == "end":
                finish(number)
            elif mark == "v" and later(number):
                continue
            else:
                still.append((number, steps))
        running = still
        tick += 1


def main_kernel(
    heads, counts_in, owners_in, hidden, queries, out_grad, nbrs, gq_in, gk_in,
    att_out, dq_out, dh_out, gains_out,
    counts, owners, gq, gk, rows_buf, kept_buf, sent_buf, stage, guest, guest_out, back, done, v_acc, total, got_line, got_plane,
    small_sem, in_sem, kept_sem, own_sem, send_sem, recv_sem, guest_send, guest_recv, back_send, back_recv, sum_send, sum_recv,
):
    c = lax.axis_index("ctx")
    m = lax.axis_index("mp")
    n = lax.axis_size("ctx")
    following, preceding = lax.rem(c + 1, n), lax.rem(c + n - 1, n)
    core, z, y = lax.rem(c, 2), lax.rem(lax.div(c, 2), 8), lax.div(c, 16)
    odd = core == 1
    columns = heads * HEAD
    moved = heads // 2
    pairs = (heads - moved) // 2

    line_at = [y * 16 + lax.rem(z + j, 8) * 2 for j in range(8)]
    y_at = [lax.rem(y + j, 4) * 16 + z * 2 for j in range(4)]
    m_at = [lax.rem(m + j, 4) for j in range(4)]

    def line(j, other):
        return (line_at[j] + other, m)

    def plane(j, other):
        return (y_at[j // 4] + other, m_at[j % 4])

    barrier = pltpu.get_barrier_semaphore()

    def greet(device):
        pl.semaphore_signal(barrier, inc=1, device_id=device, device_id_type=MESH)

    @pl.when(odd)
    def _():
        for j in (4, 3, 5, 2, 6, 1, 7):
            greet(line(j, 0))
            greet(line(j, 1))

    for j in (10, 6, 9, 11, 14, 2, 8, 5, 7, 13, 15, 1, 3, 4, 12):
        greet(plane(j, 1))
    greet((following, m))
    greet((preceding, m))
    greet((c + 1 - 2 * core, m))

    small = [
        pltpu.make_async_copy(src, dst, small_sem.at[i])
        for i, (src, dst) in enumerate(((owners_in, owners), (counts_in, counts), (gq_in, gq), (gk_in, gk)))
    ]
    for load in small:
        load.start()
    loads = [
        pltpu.make_async_copy(src, rows_buf.at[i], in_sem.at[i])
        for i, src in enumerate((hidden, queries, out_grad))
    ]
    for load in loads:
        load.start()
    half = columns // 2
    kept_loads = [
        pltpu.make_async_copy(
            nbrs.at[1, :, :, pl.ds(i * half, half)], kept_buf.at[:, :, pl.ds(i * half, half)], kept_sem.at[i]
        )
        for i in range(2)
    ]
    own_cols = pl.ds(moved * HEAD, columns - moved * HEAD)
    own_load = pltpu.make_async_copy(
        nbrs.at[0, pl.ds(0, SENT_SLOTS), :, own_cols], sent_buf.at[:, :, own_cols], own_sem
    )
    for load in kept_loads:
        load.start()

    own_load.start()
    for load in small:
        load.wait()
    gain = gq[...] * gk[...]
    lanes = lax.broadcasted_iota(jnp.int32, (1, SLOTS * NBR), 1)

    def masks(device):
        first_kept = jnp.full(lanes.shape, owners[2 * device], jnp.int32) == device
        first = jnp.full(lanes.shape, counts[2 * device] * NBR, jnp.int32)
        second = jnp.full(lanes.shape, counts[2 * device + 1] * NBR, jnp.int32)
        kept = jnp.where(lanes < jnp.where(first_kept, first, second), 1.0, 0.0)
        handed = jnp.where(lanes < jnp.where(first_kept, second, first), 1.0, 0.0)
        return kept, handed[:, : SENT_SLOTS * NBR]

    live, live_sent = masks(c)
    live_guest = masks(preceding)[1]
    for load in loads:
        load.wait()
    first_kept = jnp.full((ROWS, columns), owners[2 * c], jnp.int32) == c
    for k in range(3):
        top, bottom = rows_buf[k, :ROWS], rows_buf[k, ROWS:]
        rows_buf[k, :ROWS] = jnp.where(first_kept, top, bottom)
        handed = jnp.where(first_kept, bottom, top)
        rows_buf[k, ROWS:] = handed
        for p in range(pairs):
            at = moved * HEAD + p * PAIR
            stage[p, k] = handed[:, at : at + PAIR]
    for load in kept_loads:
        load.wait()

    sends = [
        pltpu.make_async_remote_copy(
            src_ref=nbrs.at[0, pl.ds(0, SENT_SLOTS), :, pl.ds(i * HEAD, HEAD)],
            dst_ref=sent_buf.at[:, :, pl.ds(i * HEAD, HEAD)],
            send_sem=send_sem.at[i], recv_sem=recv_sem.at[i],
            device_id=(preceding, m), device_id_type=MESH,
        )
        for i in range(moved)
    ]
    guests = [
        pltpu.make_async_remote_copy(
            src_ref=stage.at[p], dst_ref=guest.at[p], send_sem=guest_send.at[p], recv_sem=guest_recv.at[p],
            device_id=(following, m), device_id_type=MESH,
        )
        for p in range(pairs)
    ]
    backs = [
        pltpu.make_async_remote_copy(
            src_ref=guest_out.at[p], dst_ref=back.at[p], send_sem=back_send.at[p], recv_sem=back_recv.at[p],
            device_id=(preceding, m), device_id_type=MESH,
        )
        for p in range(pairs)
    ]

    def exchange():
        @pl.when(odd)
        def _():
            pl.semaphore_wait(barrier, 2 + 7 + 31)

        @pl.when(jnp.logical_not(odd))
        def _():
            pl.semaphore_wait(barrier, 2 + 8)

        for p in range(pairs):
            guests[p].start()
            for i in range(p * moved // pairs, (p + 1) * moved // pairs):
                sends[i].start()

    def kept_unit(i, result):
        if i == 0:
            exchange()
        cols = pl.ds(i * HEAD, HEAD)
        rows = [rows_buf[k, :ROWS, cols] for k in range(3)]
        return unit(kept_buf[:, :, cols].reshape(-1, HEAD), *rows, gain, live, result)

    def sent_unit(i, result):
        if 2 == 0:
            sends[i].wait_recv()
        elif i % 2 == 0:
            for k in range(i, i + 2):
                sends[k].wait_recv()
        cols = pl.ds(i * HEAD, HEAD)
        rows = [rows_buf[k, ROWS:, cols] for k in range(3)]
        return unit(sent_buf[:, :, cols].reshape(-1, HEAD), *rows, gain, live_sent, result)

    def guest_unit(i, result):
        p, r = divmod(i - moved, 2)
        if i == moved:
            own_load.wait()
        if 2 == 0 and r == 0:
            guests[p].wait_recv()
        elif 2 and i == moved:
            for k in range(pairs):
                guests[k].wait_recv()
        cols = pl.ds(i * HEAD, HEAD)
        rows = [guest[p, k, :, r * HEAD : (r + 1) * HEAD] for k in range(3)]
        return unit(sent_buf[:, :, cols].reshape(-1, HEAD), *rows, gain, live_guest, result)

    order = [(0, i) for i in range(heads)]
    order += [(2, i) for i in range(moved, heads)] + [(1, i) for i in range(moved)]
    results = [[] for _ in order]
    parked = []

    def open_unit(number):
        kind, i = order[number]
        return (kept_unit, sent_unit, guest_unit)[kind](i, results[number])

    makers = [(number, functools.partial(open_unit, number)) for number in range(len(order))]

    def finish(number):
        kind, i = order[number]
        for k in range(3):
            value = results[number][1][k]
            if kind == 2:
                p, r = divmod(i - moved, 2)
                guest_out[p, k, :, r * HEAD : (r + 1) * HEAD] = value
            else:
                done[kind, k, :, pl.ds(i * HEAD, HEAD)] = value
        if kind == 2 and r == 1:
            backs[p].start()

    def later(number):
        wait = True
        if wait:
            parked.append(number)
        return wait

    opened = {}

    def begin(number):
        opened[number] = open_unit(number)
        return opened[number]

    makers = [(number, functools.partial(begin, number)) for number in range(len(order))]
    staggered(makers[:heads], 1, finish, lambda number: False, 2)
    staggered(makers[heads:], 1, finish, later, 2)
    v_acc[...] = sum(result[0] for result in results)

    def give(src, slot, phase, device):
        pltpu.make_async_remote_copy(
            src_ref=src, dst_ref=slot, send_sem=sum_send.at[phase], recv_sem=sum_recv.at[phase],
            device_id=device, device_id_type=MESH,
        ).start()

    def settle(ref, sem):
        pltpu.make_async_copy(ref, ref, sem).wait()

    in_line, in_plane = z * 2 + core, y * 4 + m
    for j in range(1, 8):
        give(v_acc, got_line.at[in_line], 0, line(j, 1))

    @pl.when(jnp.logical_not(odd))
    def _():
        give(v_acc, got_line.at[in_line], 0, (c + 1, m))

    staggered([(number, opened[number]) for number in parked], 1, finish, lambda number: False)

    @pl.when(odd)
    def _():
        got_line[in_line] = v_acc[...]
        settle(got_line.at[pl.ds(0, 15)], sum_recv.at[0])
        total[...] = jnp.sum(got_line[...], axis=0)
        for j in range(1, 16):
            give(total, got_plane.at[in_plane], 1, plane(j, 1))
            give(total, got_plane.at[in_plane], 1, plane(j, 0))
        give(total, got_plane.at[in_plane], 1, (c - 1, m))
        got_plane[in_plane] = total[...]


    for copy in backs:
        copy.wait_recv()
    for k, out in enumerate((att_out, dq_out, dh_out)):
        for at in range(0, columns, PAIR):
            cols = slice(at, at + PAIR)
            kept = done[0, k, :, cols]
            handed = done[1, k, :, cols] if at < moved * HEAD else back[(at - moved * HEAD) // PAIR, k]
            out[:ROWS, cols] = jnp.where(first_kept[:, cols], kept, handed)
            out[ROWS:, cols] = jnp.where(first_kept[:, cols], handed, kept)
    for copy in sends + guests + backs:
        copy.wait_send()

    @pl.when(odd)
    def _():
        settle(got_line.at[pl.ds(0, 7)], sum_send.at[0])
        settle(got_plane.at[pl.ds(0, 15)], sum_recv.at[1])
        settle(got_plane.at[pl.ds(0, 15)], sum_send.at[1])
        settle(got_plane, sum_send.at[1])

    @pl.when(jnp.logical_not(odd))
    def _():
        settle(got_line.at[pl.ds(0, 8)], sum_send.at[0])
        settle(got_plane, sum_recv.at[1])

    v = jnp.sum(got_plane[...], axis=0)
    gains_out[0:1, :] = v * gk[...]
    gains_out[1:2, :] = v * gq[...]


def last_kernel(*refs):
    sources, targets, sem = refs[:4], refs[4:8], refs[8]
    stores = [
        pltpu.make_async_copy(src, dst, sem.at[i]) for i, (src, dst) in enumerate(zip(sources, targets))
    ]
    for store in stores:
        store.start()
    for store in stores:
        store.wait()


def per_device(hidden, queries, out_grad, nbrs, query_gain, key_gain, counts, owners):
    rows, columns = hidden.shape
    heads = columns // HEAD
    block = jax.ShapeDtypeStruct((rows, columns), BF16)
    vmem = pl.BlockSpec(memory_space=pltpu.VMEM)
    hbm = pl.BlockSpec(memory_space=pl.ANY)
    dma = pltpu.SemaphoreType.DMA
    gq, gk = query_gain[None], key_gain[None]
    moved = heads // 2
    pairs = (heads - moved) // 2
    results = pl.pallas_call(
        functools.partial(main_kernel, heads),
        out_shape=[pltpu.VMEM((rows, columns), BF16)] * 3 + [pltpu.VMEM((2, HEAD), F32)],
        in_specs=[hbm] * 8,
        out_specs=[vmem, vmem, vmem, vmem],
        scratch_shapes=[
            pltpu.SMEM(counts.shape, jnp.int32),
            pltpu.SMEM(counts.shape, jnp.int32),
            pltpu.VMEM((1, HEAD), F32),
            pltpu.VMEM((1, HEAD), F32),
            pltpu.VMEM((3, rows, columns), BF16),
            pltpu.VMEM((SLOTS, NBR, columns), BF16),
            pltpu.VMEM((SENT_SLOTS, NBR, columns), BF16),
            *[pltpu.VMEM((pairs, 3, ROWS, PAIR), BF16)] * 4,
            pltpu.VMEM((2, 3, ROWS, columns), BF16),
            pltpu.VMEM((1, HEAD), F32),
            pltpu.VMEM((1, HEAD), F32),
            pltpu.VMEM((16, 1, HEAD), F32),
            pltpu.VMEM((16, 1, HEAD), F32),
            dma((4,)), dma((3,)), dma((2,)), dma, dma((moved,)), dma((moved,)), dma((pairs,)), dma((pairs,)),
            dma((pairs,)), dma((pairs,)), dma((2,)), dma((2,)),
        ],
        compiler_params=pltpu.CompilerParams(
            collective_id=0, has_side_effects=True, vmem_limit_bytes=VMEM_LIMIT
        ),
    )(counts, owners, hidden, queries, out_grad, nbrs, gq, gk)
    return pl.pallas_call(
        last_kernel,
        out_shape=[block, block, block, jax.ShapeDtypeStruct((2, HEAD), F32)],
        in_specs=[vmem] * 4,
        out_specs=[hbm] * 4,
        scratch_shapes=[dma((4,))],
        compiler_params=pltpu.CompilerParams(vmem_limit_bytes=8 * 1024 * 1024),
    )(*results)


def solution(mesh):
    in_specs = (
        P("ctx", "mp"),
        P("ctx", "mp"),
        P("ctx", "mp"),
        P("ctx", None, None, "mp"),
        P(),
        P(),
        P(),
        P(),
    )
    out_specs = (P("ctx", "mp"), P("ctx", "mp"), P("ctx", "mp"), P())
    return jax.shard_map(
        per_device, mesh=mesh, in_specs=in_specs, out_specs=out_specs, check_vma=False
    )
```

time: 34.6 us -> 27.8 us (0.80)
  Pallas kernels: 33.8 us -> 27.1 us
    pallas_call x1, Pallas kernels: 30.7 us -> 26.1 us  [per_device(): pl.pallas_call(functools.partial(main_kernel, heads), out_shape=[pltpu.VM...]
    pallas_call x1, Pallas kernels: 3.12 us -> 0.91 us  [per_device(): pl.pallas_call(last_kernel, out_shape=[block, block, block, jax.ShapeDtyp...]
where the time goes in v2:
time: 27.8 us; the launch traced here: 27.7 us
  Pallas kernels  27.1 us (97%)
  between operations  0.64 us (2%)
    pallas_call x1, Pallas kernels, per_device(): pl.pallas_call(functools.partial(main_kernel, heads), out_shape=[pltpu.VM...  26.1 us
    pallas_call x1, Pallas kernels, per_device(): pl.pallas_call(last_kernel, out_shape=[block, block, block, jax.ShapeDtyp...  0.91 us

profile of v2, /device:TPU:1, one launch (start us, length us, event | category | flops | bytes accessed | tf_op | source)
XLA Modules:
  0.0 27.7 jit_solution(5178938754529405991)
XLA Ops:
  0.6 26.1 %shard_map.111 = (bf16[128,1024]{1,0:T(8,128)(2,1)S(1)}, bf16[128,1024]{1,0:T(8,128)(2,1)S(1)}, bf16[128,1024]{1,0:T(8,128)(2,1)S(1)}, f32[2,128]{1,0:T(2,128)S(1)}) custom-call(s32[128]{0:T(128)} %counts_in.1, s32[128]{0:T(128)} %owners_in.1, bf16[128,1024]{1,0:T(8,128)(2,1)} %hidden.1, bf16[128,1024]{1,0:T(8,128)(2,1)} %queries.1, ...), custom_call_target="tpu_custom_call" | custom-call | tf_op jit(solution)/shard_map/pallas_call | solution.py:416
  26.8 0.9 %shard_map.112 = (bf16[128,1024]{1,0:T(8,128)(2,1)}, bf16[128,1024]{1,0:T(8,128)(2,1)}, bf16[128,1024]{1,0:T(8,128)(2,1)}, f32[2,128]{1,0:T(2,128)}) custom-call(bf16[128,1024]{1,0:T(8,128)(2,1)S(1)} %get-tuple-element.8.refs_0_, bf16[128,1024]{1,0:T(8,128)(2,1)S(1)} %get-tuple-element.9.refs_1_, bf16[128,1024]{1,0:T(8,128)(2,1)S(1)} %get-tuple-element.10.refs_2_, ...), custom_call_target="tpu_custom_call" | custom-call | tf_op jit(solution)/shard_map/pallas_call | solution.py:442

commit v3 on v2

--- a/solution.py
+++ b/solution.py
@@ -17,6 +17,7 @@
 EPSILON = 1e-06
 SCALE = 1.0 / math.sqrt(HEAD)
 LOG2E = math.log2(math.e)
+FAR_FIRST = (10, 6, 9, 11, 14, 2, 8, 5, 7, 13, 15, 1, 3, 4, 12)
 MESH = pl.DeviceIdType.MESH
 VMEM_LIMIT = 63 * 1024 * 1024
 BF16 = jnp.bfloat16
@@ -46,28 +47,43 @@
     return (value.reshape(-1, k, value.shape[1]) * row[None]).reshape(value.shape)
 
 
-def unit(x, h, q, g, gain, live, result):
+def unit(get_x, get_rows, x_first, gain, live, result):
     eye = (
         lax.broadcasted_iota(jnp.int32, (HEAD, HEAD), 0)
         == lax.broadcasted_iota(jnp.int32, (HEAD, HEAD), 1)
     ).astype(BF16)
     ones = jnp.ones((16, HEAD), BF16)
     root = math.sqrt(HEAD)
-    xt = jnp.transpose(x)
-    hf, qf = h.astype(F32), q.astype(F32)
-    rh = lax.rsqrt(jnp.sum(hf * hf, axis=1, keepdims=True) + HEAD * EPSILON)
-    rq = lax.rsqrt(jnp.sum(qf * qf, axis=1, keepdims=True) + HEAD * EPSILON)
-    hn, qn = hf * rh, qf * rq
-    ek = (hn * gain).astype(BF16)
-    qg = jnp.concatenate([qn.astype(BF16), g], axis=0)
-    rx = lax.rsqrt(mm(ones, xt * xt) + HEAD * EPSILON)
+
+    def from_x(x):
+        xt = jnp.transpose(x)
+        return x, xt, lax.rsqrt(mm(ones, xt * xt) + HEAD * EPSILON)
+
+    def from_rows(h, q, g):
+        hf, qf = h.astype(F32), q.astype(F32)
+        rh = lax.rsqrt(jnp.sum(hf * hf, axis=1, keepdims=True) + HEAD * EPSILON)
+        rq = lax.rsqrt(jnp.sum(qf * qf, axis=1, keepdims=True) + HEAD * EPSILON)
+        hn, qn = hf * rh, qf * rq
+        qg = jnp.concatenate([qn.astype(BF16), g], axis=0)
+        mix = jnp.concatenate([eye, jnp.transpose(h)], axis=1)
+        back_mix = jnp.concatenate([jnp.transpose(qg), eye], axis=1)
+        return h, rh, rq, hn, qn, qg, mix, back_mix, (hn * gain).astype(BF16)
+
+    if x_first:
+        x, xt, rx = from_x(get_x())
+        yield "pre"
+        h, rh, rq, hn, qn, qg, mix, back_mix, ek = from_rows(*get_rows())
+    else:
+        h, rh, rq, hn, qn, qg, mix, back_mix, ek = from_rows(*get_rows())
+        yield "pre"
+        x, xt, rx = from_x(get_x())
     yield
     s = mm(ek, xt)
     yield
     p = jnp.exp2(over_rows(s, rx[:8] * (root * LOG2E)))
     wb = (p * (1.0 / jnp.sum(p, axis=0, keepdims=True))).astype(BF16)
     yield
-    eb = mm(jnp.concatenate([eye, jnp.transpose(h)], axis=1), jnp.concatenate([xt, wb], axis=0)).astype(BF16)
+    eb = mm(mix, jnp.concatenate([xt, wb], axis=0)).astype(BF16)
     yield
     both = mm(qg, eb)
     re = lax.rsqrt(mm(ones, eb * eb) + HEAD * EPSILON)
@@ -78,19 +94,18 @@
     inv = 1.0 / jnp.sum(p, axis=1, keepdims=True)
     shift = jnp.sum(p * da, axis=1, keepdims=True) * inv
     ab = (p * inv).astype(BF16)
-    dt = over_rows(ab * (da - shift).astype(BF16), (re * root).astype(BF16))
+    dtf = over_rows(p * inv * (da - shift), re[:8] * root)
+    dt = dtf.astype(BF16)
     ta = jnp.concatenate([dt, ab], axis=0)
     yield
-    c = mm(ones[:, :ROWS], dt * t.astype(BF16)) * (re * re)
+    c = jnp.sum(dtf * t, axis=0, keepdims=True) * (re * re)
     ec = over_rows(eb, (-c).astype(BF16))
     yield
-    deb = mm(jnp.concatenate([jnp.transpose(qg), eye], axis=1), jnp.concatenate([ta, ec], axis=0)).astype(BF16)
+    deb = mm(back_mix, jnp.concatenate([ta, ec], axis=0)).astype(BF16)
     yield
     dw = mm(h, deb)
     yield
-    dk = mm(ones[:, :ROWS], wb * dw.astype(BF16))
-    ds = wb * (dw.reshape(-1, 8, dw.shape[1]) - dk[None, :8]).reshape(dw.shape).astype(BF16)
-    yield
+    ds = wb * (dw - jnp.sum(wb.astype(F32) * dw, axis=0, keepdims=True)).astype(BF16)
     ux = mm(over_rows(ds, (rx * root).astype(BF16)), x)
     yield
     u = ux * hn
@@ -117,7 +132,7 @@
             mark = next(steps, "end")
             if mark == "end":
                 finish(number)
-            elif mark == "v" and later(number):
+            elif mark in ("pre", "v") and later(number, mark):
                 continue
             else:
                 still.append((number, steps))
@@ -162,7 +177,7 @@
             greet(line(j, 0))
             greet(line(j, 1))
 
-    for j in (10, 6, 9, 11, 14, 2, 8, 5, 7, 13, 15, 1, 3, 4, 12):
+    for j in FAR_FIRST:
         greet(plane(j, 1))
     greet((following, m))
     greet((preceding, m))
@@ -221,8 +236,13 @@
         for p in range(pairs):
             at = moved * HEAD + p * PAIR
             stage[p, k] = handed[:, at : at + PAIR]
-    for load in kept_loads:
-        load.wait()
+    @pl.when(odd)
+    def _():
+        pl.semaphore_wait(barrier, 2 + 7 + 31)
+
+    @pl.when(jnp.logical_not(odd))
+    def _():
+        pl.semaphore_wait(barrier, 2 + 8)
 
     sends = [
         pltpu.make_async_remote_copy(
@@ -233,6 +253,8 @@
         )
         for i in range(moved)
     ]
+    for copy in sends:
+        copy.start()
     guests = [
         pltpu.make_async_remote_copy(
             src_ref=stage.at[p], dst_ref=guest.at[p], send_sem=guest_send.at[p], recv_sem=guest_recv.at[p],
@@ -248,52 +270,43 @@
         for p in range(pairs)
     ]
 
-    def exchange():
-        @pl.when(odd)
-        def _():
-            pl.semaphore_wait(barrier, 2 + 7 + 31)
-
-        @pl.when(jnp.logical_not(odd))
-        def _():
-            pl.semaphore_wait(barrier, 2 + 8)
-
-        for p in range(pairs):
-            guests[p].start()
-            for i in range(p * moved // pairs, (p + 1) * moved // pairs):
-                sends[i].start()
+    for copy in guests:
+        copy.start()
+    for load in kept_loads:
+        load.wait()
+
+
+    def block(buf, i):
+        return buf[:, :, pl.ds(i * HEAD, HEAD)].reshape(-1, HEAD)
+
+    def own_rows(first, i):
+        return [rows_buf[k, first : first + ROWS, pl.ds(i * HEAD, HEAD)] for k in range(3)]
 
     def kept_unit(i, result):
-        if i == 0:
-            exchange()
-        cols = pl.ds(i * HEAD, HEAD)
-        rows = [rows_buf[k, :ROWS, cols] for k in range(3)]
-        return unit(kept_buf[:, :, cols].reshape(-1, HEAD), *rows, gain, live, result)
+        return unit(lambda: block(kept_buf, i), lambda: own_rows(0, i), False, gain, live, result)
 
     def sent_unit(i, result):
-        if 2 == 0:
-            sends[i].wait_recv()
-        elif i % 2 == 0:
-            for k in range(i, i + 2):
-                sends[k].wait_recv()
-        cols = pl.ds(i * HEAD, HEAD)
-        rows = [rows_buf[k, ROWS:, cols] for k in range(3)]
-        return unit(sent_buf[:, :, cols].reshape(-1, HEAD), *rows, gain, live_sent, result)
+        def arrived():
+            if i % 2 == 0:
+                sends[i].wait_recv()
+                sends[i + 1].wait_recv()
+            return block(sent_buf, i)
+
+        return unit(arrived, lambda: own_rows(ROWS, i), False, gain, live_sent, result)
 
     def guest_unit(i, result):
         p, r = divmod(i - moved, 2)
-        if i == moved:
-            own_load.wait()
-        if 2 == 0 and r == 0:
-            guests[p].wait_recv()
-        elif 2 and i == moved:
-            for k in range(pairs):
-                guests[k].wait_recv()
-        cols = pl.ds(i * HEAD, HEAD)
-        rows = [guest[p, k, :, r * HEAD : (r + 1) * HEAD] for k in range(3)]
-        return unit(sent_buf[:, :, cols].reshape(-1, HEAD), *rows, gain, live_guest, result)
+
+        def arrived():
+            if r == 0:
+                guests[p].wait_recv()
+            return [guest[p, k, :, r * HEAD : (r + 1) * HEAD] for k in range(3)]
+
+        return unit(lambda: block(sent_buf, i), arrived, True, gain, live_guest, result)
 
     order = [(0, i) for i in range(heads)]
-    order += [(2, i) for i in range(moved, heads)] + [(1, i) for i in range(moved)]
+    for p in range(pairs):
+        order += [(1, 2 * p), (1, 2 * p + 1), (2, moved + 2 * p), (2, moved + 2 * p + 1)]
     results = [[] for _ in order]
     parked = []
 
@@ -315,12 +328,6 @@
         if kind == 2 and r == 1:
             backs[p].start()
 
-    def later(number):
-        wait = True
-        if wait:
-            parked.append(number)
-        return wait
-
     opened = {}
 
     def begin(number):
@@ -328,8 +335,22 @@
         return opened[number]
 
     makers = [(number, functools.partial(begin, number)) for number in range(len(order))]
-    staggered(makers[:heads], 1, finish, lambda number: False, 2)
-    staggered(makers[heads:], 1, finish, later, 2)
+    ready = []
+
+    def hold(number, mark):
+        held = number >= heads and mark == "pre"
+        if held:
+            ready.append((number, opened[number]))
+        return held
+
+    def park(number, mark):
+        if mark == "v":
+            parked.append(number)
+        return mark == "v"
+
+    own_load.wait()
+    staggered(makers, 1, finish, hold, 2)
+    staggered(ready, 1, finish, park, 2)
     v_acc[...] = sum(result[0] for result in results)
 
     def give(src, slot, phase, device):
@@ -342,23 +363,23 @@
         pltpu.make_async_copy(ref, ref, sem).wait()
 
     in_line, in_plane = z * 2 + core, y * 4 + m
-    for j in range(1, 8):
+    for j in (4, 3, 5, 2, 6, 1, 7):
         give(v_acc, got_line.at[in_line], 0, line(j, 1))
 
     @pl.when(jnp.logical_not(odd))
     def _():
         give(v_acc, got_line.at[in_line], 0, (c + 1, m))
 
-    staggered([(number, opened[number]) for number in parked], 1, finish, lambda number: False)
+    staggered([(number, opened[number]) for number in parked], 1, finish, park)
 
     @pl.when(odd)
     def _():
         got_line[in_line] = v_acc[...]
         settle(got_line.at[pl.ds(0, 15)], sum_recv.at[0])
         total[...] = jnp.sum(got_line[...], axis=0)
-        for j in range(1, 16):
+        for j in FAR_FIRST:
+            give(total, got_plane.at[in_plane], 1, plane(j, 0))
             give(total, got_plane.at[in_plane], 1, plane(j, 1))
-            give(total, got_plane.at[in_plane], 1, plane(j, 0))
         give(total, got_plane.at[in_plane], 1, (c - 1, m))
         got_plane[in_plane] = total[...]
 

time: 27.8 us -> 27.2 us (0.978)
  Pallas kernels: 27.1 us -> 26.5 us
    pallas_call x1, Pallas kernels: 26.1 us -> 25.6 us  [per_device(): pl.pallas_call(functools.partial(main_kernel, heads), out_shape=[pltpu.VM...]
where the time goes in v3:
time: 27.2 us; the launch traced here: 27.1 us
  Pallas kernels  26.5 us (97%)
  between operations  0.64 us (2%)
    pallas_call x1, Pallas kernels, per_device(): pl.pallas_call(functools.partial(main_kernel, heads), out_shape=[pltpu.VM...  25.6 us
    pallas_call x1, Pallas kernels, per_device(): pl.pallas_call(last_kernel, out_shape=[block, block, block, jax.ShapeDtyp...  0.91 us

profile of v3, /device:TPU:1, one launch (start us, length us, event | category | flops | bytes accessed | tf_op | source)
XLA Modules:
  0.0 27.1 jit_solution(12295543809102767171)
XLA Ops:
  0.6 25.6 %shard_map.111 = (bf16[128,1024]{1,0:T(8,128)(2,1)S(1)}, bf16[128,1024]{1,0:T(8,128)(2,1)S(1)}, bf16[128,1024]{1,0:T(8,128)(2,1)S(1)}, f32[2,128]{1,0:T(2,128)S(1)}) custom-call(s32[128]{0:T(128)} %counts_in.1, s32[128]{0:T(128)} %owners_in.1, bf16[128,1024]{1,0:T(8,128)(2,1)} %hidden.1, bf16[128,1024]{1,0:T(8,128)(2,1)} %queries.1, ...), custom_call_target="tpu_custom_call" | custom-call | tf_op jit(solution)/shard_map/pallas_call | solution.py:437
  26.2 0.9 %shard_map.112 = (bf16[128,1024]{1,0:T(8,128)(2,1)}, bf16[128,1024]{1,0:T(8,128)(2,1)}, bf16[128,1024]{1,0:T(8,128)(2,1)}, f32[2,128]{1,0:T(2,128)}) custom-call(bf16[128,1024]{1,0:T(8,128)(2,1)S(1)} %get-tuple-element.8.refs_0_, bf16[128,1024]{1,0:T(8,128)(2,1)S(1)} %get-tuple-element.9.refs_1_, bf16[128,1024]{1,0:T(8,128)(2,1)S(1)} %get-tuple-element.10.refs_2_, ...), custom_call_target="tpu_custom_call" | custom-call | tf_op jit(solution)/shard_map/pallas_call | solution.py:463

commit v4 on v3

--- a/solution.py
+++ b/solution.py
@@ -306,7 +306,7 @@
 
     order = [(0, i) for i in range(heads)]
     for p in range(pairs):
-        order += [(1, 2 * p), (1, 2 * p + 1), (2, moved + 2 * p), (2, moved + 2 * p + 1)]
+        order += [(2, moved + 2 * p), (2, moved + 2 * p + 1), (1, 2 * p), (1, 2 * p + 1)]
     results = [[] for _ in order]
     parked = []
 
@@ -350,7 +350,7 @@
 
     own_load.wait()
     staggered(makers, 1, finish, hold, 2)
-    staggered(ready, 1, finish, park, 2)
+    staggered(ready, 4, finish, park, 4)
     v_acc[...] = sum(result[0] for result in results)
 
     def give(src, slot, phase, device):

time: 27.2 us -> 26.6 us (0.978)
  Pallas kernels: 26.5 us -> 25.8 us
    pallas_call x1, Pallas kernels: 25.6 us -> 24.9 us  [per_device(): pl.pallas_call(functools.partial(main_kernel, heads), out_shape=[pltpu.VM...]
where the time goes in v4:
time: 26.6 us; the launch traced here: 26.5 us
  Pallas kernels  25.8 us (97%)
  between operations  0.64 us (2%)
    pallas_call x1, Pallas kernels, per_device(): pl.pallas_call(functools.partial(main_kernel, heads), out_shape=[pltpu.VM...  24.9 us
    pallas_call x1, Pallas kernels, per_device(): pl.pallas_call(last_kernel, out_shape=[block, block, block, jax.ShapeDtyp...  0.91 us

profile of v4, /device:TPU:1, one launch (start us, length us, event | category | flops | bytes accessed | tf_op | source)
XLA Modules:
  0.0 26.5 jit_solution(2051236873517997648)
XLA Ops:
  0.6 24.9 %shard_map.111 = (bf16[128,1024]{1,0:T(8,128)(2,1)S(1)}, bf16[128,1024]{1,0:T(8,128)(2,1)S(1)}, bf16[128,1024]{1,0:T(8,128)(2,1)S(1)}, f32[2,128]{1,0:T(2,128)S(1)}) custom-call(s32[128]{0:T(128)} %counts_in.1, s32[128]{0:T(128)} %owners_in.1, bf16[128,1024]{1,0:T(8,128)(2,1)} %hidden.1, bf16[128,1024]{1,0:T(8,128)(2,1)} %queries.1, ...), custom_call_target="tpu_custom_call" | custom-call | tf_op jit(solution)/shard_map/pallas_call | solution.py:437
  25.6 0.9 %shard_map.112 = (bf16[128,1024]{1,0:T(8,128)(2,1)}, bf16[128,1024]{1,0:T(8,128)(2,1)}, bf16[128,1024]{1,0:T(8,128)(2,1)}, f32[2,128]{1,0:T(2,128)}) custom-call(bf16[128,1024]{1,0:T(8,128)(2,1)S(1)} %get-tuple-element.8.refs_0_, bf16[128,1024]{1,0:T(8,128)(2,1)S(1)} %get-tuple-element.9.refs_1_, bf16[128,1024]{1,0:T(8,128)(2,1)S(1)} %get-tuple-element.10.refs_2_, ...), custom_call_target="tpu_custom_call" | custom-call | tf_op jit(solution)/shard_map/pallas_call | solution.py:463

commit v5 on v4

--- a/solution.py
+++ b/solution.py
@@ -285,21 +285,20 @@
     def kept_unit(i, result):
         return unit(lambda: block(kept_buf, i), lambda: own_rows(0, i), False, gain, live, result)
 
+    def arrive(p):
+        guests[p].wait_recv()
+        for i in range(2 * p, 2 * p + 2):
+            sends[i].wait_recv()
+
     def sent_unit(i, result):
-        def arrived():
-            if i % 2 == 0:
-                sends[i].wait_recv()
-                sends[i + 1].wait_recv()
-            return block(sent_buf, i)
-
-        return unit(arrived, lambda: own_rows(ROWS, i), False, gain, live_sent, result)
+        return unit(lambda: block(sent_buf, i), lambda: own_rows(ROWS, i), False, gain, live_sent, result)
 
     def guest_unit(i, result):
         p, r = divmod(i - moved, 2)
 
         def arrived():
             if r == 0:
-                guests[p].wait_recv()
+                arrive(p)
             return [guest[p, k, :, r * HEAD : (r + 1) * HEAD] for k in range(3)]
 
         return unit(lambda: block(sent_buf, i), arrived, True, gain, live_guest, result)
@@ -349,7 +348,7 @@
         return mark == "v"
 
     own_load.wait()
-    staggered(makers, 1, finish, hold, 2)
+    staggered(makers, 2, finish, hold, 4)
     staggered(ready, 4, finish, park, 4)
     v_acc[...] = sum(result[0] for result in results)
 

time: 26.6 us -> 26.6 us (level)
  no operation moved by 1% of the time
where the time goes in v5:
time: 26.6 us; the launch traced here: 26.5 us
  Pallas kernels  25.8 us (97%)
  between operations  0.64 us (2%)
    pallas_call x1, Pallas kernels, per_device(): pl.pallas_call(functools.partial(main_kernel, heads), out_shape=[pltpu.VM...  24.9 us
    pallas_call x1, Pallas kernels, per_device(): pl.pallas_call(last_kernel, out_shape=[block, block, block, jax.ShapeDtyp...  0.91 us

profile of v5, /device:TPU:1, one launch (start us, length us, event | category | flops | bytes accessed | tf_op | source)
XLA Modules:
  0.0 26.5 jit_solution(5787417888424867948)
XLA Ops:
  0.6 24.9 %shard_map.111 = (bf16[128,1024]{1,0:T(8,128)(2,1)S(1)}, bf16[128,1024]{1,0:T(8,128)(2,1)S(1)}, bf16[128,1024]{1,0:T(8,128)(2,1)S(1)}, f32[2,128]{1,0:T(2,128)S(1)}) custom-call(s32[128]{0:T(128)} %counts_in.1, s32[128]{0:T(128)} %owners_in.1, bf16[128,1024]{1,0:T(8,128)(2,1)} %hidden.1, bf16[128,1024]{1,0:T(8,128)(2,1)} %queries.1, ...), custom_call_target="tpu_custom_call" | custom-call | tf_op jit(solution)/shard_map/pallas_call | solution.py:436
  25.6 0.9 %shard_map.112 = (bf16[128,1024]{1,0:T(8,128)(2,1)}, bf16[128,1024]{1,0:T(8,128)(2,1)}, bf16[128,1024]{1,0:T(8,128)(2,1)}, f32[2,128]{1,0:T(2,128)}) custom-call(bf16[128,1024]{1,0:T(8,128)(2,1)S(1)} %get-tuple-element.8.refs_0_, bf16[128,1024]{1,0:T(8,128)(2,1)S(1)} %get-tuple-element.9.refs_1_, bf16[128,1024]{1,0:T(8,128)(2,1)S(1)} %get-tuple-element.10.refs_2_, ...), custom_call_target="tpu_custom_call" | custom-call | tf_op jit(solution)/shard_map/pallas_call | solution.py:462
